TPU v7x, 32 devices: a whole 2x2x4 slice. The times are simulated.
32 devices in a mesh: dp: 2 (over x), mx: 4 (over z), my: 4 (over y, core).
Axes of the slice: x: 2, y: 2, z: 4, core: 2. Of those that a mesh axis runs over, the one named last changes fastest.
Arguments:
- inputs: bfloat16 [2048, 6144], P(('dp', 'my'), 'mx'), may hold values from -6 to 6
- hidden_in: bfloat16 [2048, 24576], P(('dp', 'mx'), 'my'), may hold values from -6 to 6
- out_grad: bfloat16 [2048, 6144], P(('dp', 'my'), 'mx'), may hold values from -6 to 6
- up_weight: bfloat16 [6144, 24576], P('mx', 'my'), may hold values from -0.078125 to 0.078125
- down_weight: bfloat16 [24576, 6144], P('my', 'mx'), may hold values from -0.0390625 to 0.0390625
Outputs:
- inputs_grad: bfloat16 [2048, 6144], P(('dp', 'my'), 'mx')
- up_grad: bfloat16 [6144, 24576], P('mx', 'my')
- down_grad: bfloat16 [24576, 6144], P('my', 'mx')
All inputs are finite; a program needn't handle non-finite values.
Results may differ from a plain program's by a relative error of at most 0.0059.
Values may be sent and summed in bfloat16 or wider, within the bound.
A program may use at most 192 MiB of HBM per device.

v0:
```python
import jax
import jax.numpy as jnp
from jax import lax
from jax.sharding import PartitionSpec as P


def gelu_value(value):
    return 0.5 * value * (1.0 + lax.erf(value * 0.7071067811865476))


def gelu_slope(value):
    return (
        0.5 * (1.0 + lax.erf(value * 0.7071067811865476))
        + value * jnp.exp(-0.5 * value * value) * 0.3989422804014327
    )


def per_device(inputs, hidden_in, out_grad, up_weight, down_weight):
    total_tokens = out_grad.shape[0] * lax.axis_size("my") * lax.axis_size("dp")
    grad_scale = 1.0 / jnp.sqrt(jnp.float32(total_tokens))
    pre_value = hidden_in.astype(jnp.float32)
    act_local = gelu_value(pre_value).astype(jnp.bfloat16)
    act_whole = lax.all_gather(act_local, "mx", axis=0, tiled=True)
    input_whole, grad_whole = (
        lax.all_gather(inputs, "my", axis=0, tiled=True),
        lax.all_gather(out_grad, "my", axis=0, tiled=True),
    )
    down_part = (
        jnp.einsum("tf,td->fd", act_whole, grad_whole, preferred_element_type=jnp.float32)
        * grad_scale
    )
    row_block = grad_whole
    act_grad = lax.psum_scatter(
        jnp.einsum("td,fd->tf", row_block, down_weight, preferred_element_type=jnp.float32),
        "mx",
        scatter_dimension=0,
        tiled=True,
    )
    pre_grad = (act_grad * gelu_slope(pre_value)).astype(jnp.bfloat16)
    pre_whole = lax.all_gather(pre_grad, "mx", axis=0, tiled=True)
    row_block = pre_whole
    inputs_grad = lax.psum_scatter(
        jnp.einsum("tf,df->td", row_block, up_weight, preferred_element_type=jnp.float32),
        "my",
        scatter_dimension=0,
        tiled=True,
    ).astype(jnp.bfloat16)
    up_part = (
        jnp.einsum("td,tf->df", input_whole, pre_whole, preferred_element_type=jnp.float32)
        * grad_scale
    )
    up_total, down_total = (
        lax.psum(up_part.astype(jnp.bfloat16), "dp").astype(jnp.float32),
        lax.psum(down_part.astype(jnp.bfloat16), "dp").astype(jnp.float32),
    )
    return (inputs_grad, up_total.astype(jnp.bfloat16), down_total.astype(jnp.bfloat16))


def solution(mesh):
    return jax.shard_map(
        per_device,
        mesh=mesh,
        in_specs=(
            P(("dp", "my"), "mx"),
            P(("dp", "mx"), "my"),
            P(("dp", "my"), "mx"),
            P("mx", "my"),
            P("my", "mx"),
        ),
        out_specs=(P(("dp", "my"), "mx"), P("mx", "my"), P("my", "mx")),
        check_vma=False,
    )
```

profile of v0, /device:TPU:0, one launch (start us, length us, event | category | flops | bytes accessed | tf_op | source)
XLA Modules:
  0.0 1898.0 jit_solution(14674259792016940110)
XLA Ops:
  7.2 0.0 all-gather.5.cloned.1.call-start
  7.2 0.7 all-gather.5.cloned.1.call-update
  7.9 0.0 reduce-scatter.3.cloned.1.call-start
  7.9 32.9 %all-gather.5.cloned.1.call-done = bf16[1024,1536]{1,0:T(8,128)(2,1)} async-done(((bf16[256,1536]{1,0:T(8,128)(2,1)}), bf16[1024,1536]{1,0:T(8,128)(2,1)}) %all-gather.5.cloned.1.call-update) | async-done | bytes 3145744 | tf_op jit(solution)/shard_map/all_gather | solution.py:26
  40.8 26.3 %fusion.10 = f32[1024,6144]{1,0:T(8,128)} fusion(bf16[1024,1536]{1,0:T(8,128)(2,1)} %all-gather.5.cloned.1.call-done, bf16[6144,1536]{1,0:T(8,128)(2,1)} %param.9), kind=kOutput, calls=%fused_computation.17 | convolution fusion | flops 19327352832 | bytes 47185920 | tf_op jit(solution)/shard_map/td,fd->tf/dot_general | solution.py:34
  67.1 0.0 copy-start
  67.1 0.0 reduce-scatter.3.cloned.1.call-update
  67.1 0.0 all-gather.7.cloned.1.call-start
  67.2 414.5 %reduce-scatter.3.cloned.1.call-done = f32[256,6144]{1,0:T(8,128)} async-done(((f32[1024,6144]{1,0:T(8,128)}), f32[256,6144]{1,0:T(8,128)}) %reduce-scatter.3.cloned.1.call-update) | async-done | bytes 6291472 | tf_op jit(solution)/shard_map/reduce_scatter | solution.py:33
  481.7 0.0 copy-done
  481.7 8.1 fusion.9
  489.8 0.0 all-gather.7.cloned.1.call-update
  489.8 0.0 all-gather.11.cloned.1.call-start
  489.9 0.5 all-gather.11.cloned.1.call-update
  490.4 0.0 all-gather.9.cloned.1.call-start
  490.5 0.5 all-gather.9.cloned.1.call-update
  491.0 0.0 reduce-scatter.5.cloned.1.call-start
  491.1 219.0 %all-gather.7.cloned.1.call-done = bf16[1024,6144]{1,0:T(8,128)(2,1)} async-done(((bf16[256,6144]{1,0:T(8,128)(2,1)}), bf16[1024,6144]{1,0:T(8,128)(2,1)}) %all-gather.7.cloned.1.call-update) | async-done | bytes 12582928 | tf_op jit(solution)/shard_map/all_gather | solution.py:40
  710.0 26.4 %fusion.11 = f32[1024,1536]{1,0:T(8,128)} fusion(bf16[1024,6144]{1,0:T(8,128)(2,1)} %all-gather.7.cloned.1.call-done, bf16[1536,6144]{1,0:T(8,128)(2,1)} %param.8), kind=kOutput, calls=%fused_computation.18 | convolution fusion | flops 19327352832 | bytes 37748736 | tf_op jit(solution)/shard_map/tf,df->td/dot_general | solution.py:43
  736.4 0.0 copy-start.1
  736.4 0.0 reduce-scatter.5.cloned.1.call-update
  736.4 0.2 all-reduce.3.cloned.1.call-start
  736.7 191.9 %all-gather.11.cloned.1.call-done = bf16[1024,6144]{1,0:T(8,128)(2,1)} async-done(((bf16[256,6144]{1,0:T(8,128)(2,1)}), bf16[1024,6144]{1,0:T(8,128)(2,1)}) %all-gather.11.cloned.1.call-update) | async-done | bytes 12582928 | tf_op jit(solution)/shard_map/all_gather | solution.py:23
  928.5 0.0 copy-done.1
  928.5 28.4 %multiply_convert_fusion = bf16[6144,1536]{1,0:T(8,128)(2,1)} fusion(bf16[1024,6144]{1,0:T(8,128)(2,1)} %all-gather.11.cloned.1.call-done, bf16[1024,1536]{1,0:T(8,128)(2,1)S(1)} %copy-done.1), kind=kOutput, calls=%fused_computation | convolution fusion | flops 19346227200 | bytes 34603008 | tf_op jit(solution)/shard_map/tf,td->fd/dot_general | solution.py:29
  956.9 0.0 all-gather.9.cloned.1.call-done
  956.9 27.9 %fusion = bf16[1536,6144]{0,1:T(8,128)(2,1)} fusion(bf16[1024,6144]{1,0:T(8,128)(2,1)} %all-gather.7.cloned.1.call-done, bf16[1024,1536]{1,0:T(8,128)(2,1)} %all-gather.9.cloned.1.call-done), kind=kOutput, calls=%fused_computation.2 | convolution fusion | flops 19346227200 | bytes 34603008 | tf_op jit(solution)/shard_map/td,tf->df/dot_general | solution.py:49
  984.8 0.0 all-reduce.3.cloned.1.call-update
  984.9 32.9 %reduce-scatter.5.cloned.1.call-done = f32[256,1536]{1,0:T(8,128)} async-done(((f32[1024,1536]{1,0:T(8,128)}), f32[256,1536]{1,0:T(8,128)}) %reduce-scatter.5.cloned.1.call-update) | async-done | bytes 1572880 | tf_op jit(solution)/shard_map/reduce_scatter | solution.py:42
  1017.7 2.4 convert_element_type.27
  1020.1 830.1 %all-reduce.3.cloned.1.call-done = (bf16[1536,6144]{0,1:T(8,128)(2,1)}, bf16[6144,1536]{1,0:T(8,128)(2,1)}) async-done(((bf16[1536,6144]{0,1:T(8,128)(2,1)}, bf16[6144,1536]{1,0:T(8,128)(2,1)}), (bf16[1536,6144]{0,1:T(8,128)(2,1)}, bf16[6144,1536]{1,0:T(8,128)(2,1)})) %all-reduce.3.cloned.1.call-update) | async-done | bytes 37748752 | tf_op jit(solution)/shard_map/psum | solution.py:53
  1850.2 24.6 %copy.8 = bf16[1536,6144]{1,0:T(8,128)(2,1)} copy(bf16[1536,6144]{0,1:T(8,128)(2,1)} %get-tuple-element.6) | data formatting | bytes 37748736
  1874.7 16.5 copy.11
Async XLA Ops:
  7.2 33.7 %all-gather.5.cloned.1.call-start = ((), (), s32[]{:S(2)}) async-start(), calls=%async_computation.2 | async-start | bytes 3932160 | tf_op jit(solution)/shard_map/all_gather | solution.py:26
  7.9 473.8 %reduce-scatter.3.cloned.1.call-start = ((), (), s32[]{:S(2)}) async-start(), calls=%async_computation.3 | async-start | bytes 31457280 | tf_op jit(solution)/shard_map/reduce_scatter | solution.py:33
  67.1 414.6 %copy-start = (bf16[256,6144]{1,0:T(8,128)(2,1)S(1)}, bf16[256,6144]{1,0:T(8,128)(2,1)}, u32[]{:S(2)}) copy-start(bf16[256,6144]{1,0:T(8,128)(2,1)} %param.6) | copy-start | bytes 9437188
  67.1 642.9 %all-gather.7.cloned.1.call-start = ((), (), s32[]{:S(2)}) async-start(), calls=%async_computation.4 | async-start | bytes 15728640 | tf_op jit(solution)/shard_map/all_gather | solution.py:40
  489.8 438.7 %all-gather.11.cloned.1.call-start = ((), (), s32[]{:S(2)}) async-start(), calls=%async_computation.7 | async-start | bytes 15728640 | tf_op jit(solution)/shard_map/all_gather | solution.py:23
  490.4 466.5 %all-gather.9.cloned.1.call-start = ((), (), s32[]{:S(2)}) async-start(), calls=%async_computation.6 | async-start | bytes 3932160 | tf_op jit(solution)/shard_map/all_gather | solution.py:25
  491.0 526.7 %reduce-scatter.5.cloned.1.call-start = ((), (), s32[]{:S(2)}) async-start(), calls=%async_computation.5 | async-start | bytes 7864320 | tf_op jit(solution)/shard_map/reduce_scatter | solution.py:42
  736.4 192.1 %copy-start.1 = (bf16[1024,1536]{1,0:T(8,128)(2,1)S(1)}, bf16[1024,1536]{1,0:T(8,128)(2,1)}, u32[]{:S(2)}) copy-start(bf16[1024,1536]{1,0:T(8,128)(2,1)} %all-gather.5.cloned.1.call-done) | copy-start | bytes 9437188
  736.4 1113.7 %all-reduce.3.cloned.1.call-start = ((), (), s32[]{:S(2)}) async-start(), calls=%async_computation.8 | async-start | bytes 75497472 | tf_op jit(solution)/shard_map/psum | solution.py:53
Sparse Core Ops, SparseCore 0:
  9.6 31.2 all-gather.4
  67.3 414.3 reduce-scatter.2
  490.0 220.0 all-gather.6
  712.1 216.3 all-gather.10
  930.0 26.7 all-gather.8
  959.3 58.3 reduce-scatter.4
  1020.8 829.2 all-reduce.2
where the time goes:
time: 1900 us
  waiting for transfers between devices  1720 us (91%)
  matrix products  109 us (6%)
  local copies, waits for them, and re-layouts  41 us (2%)
    psum x1, waiting for transfers between devices, per_device(): lax.psum(up_part.astype(jnp.bfloat16), 'dp').astype(jnp.float32)  830 us
    reduce_scatter x1, waiting for transfers between devices, per_device(): lax.psum_scatter(jnp.einsum('td,fd->tf', row_block, down_weight, preferre...  414 us
    all_gather x1, waiting for transfers between devices, per_device(): pre_whole = lax.all_gather(pre_grad, 'mx', axis=0, tiled=True)  219 us
    all_gather x1, waiting for transfers between devices, per_device(): act_whole = lax.all_gather(act_local, 'mx', axis=0, tiled=True)  192 us
    unnamed x6, local copies, waits for them, and re-layouts  41 us
  transfers between devices with their start and end apart: 7, of which 6 were waited for; matrix products, arithmetic and copies ran while one was open for 4% of the time, Pallas kernels for 0%

commit v1 on v0

v1 whole, which is shorter than its diff:
```python
import jax
import jax.numpy as jnp
from jax import lax
from jax.sharding import PartitionSpec as P

BF16, F32 = jnp.bfloat16, jnp.float32


def gelu_value(value):
    return 0.5 * value * (1.0 + lax.erf(value * 0.7071067811865476))


def gelu_slope(value):
    return (
        0.5 * (1.0 + lax.erf(value * 0.7071067811865476))
        + value * jnp.exp(-0.5 * value * value) * 0.3989422804014327
    )


def swap(block):
    return lax.ppermute(block, "dp", [(0, 1), (1, 0)])


def add(first, *others):
    total = first.astype(F32)
    for other in others:
        total = total + other.astype(F32)
    return total


def after(value, *earlier):
    for other in earlier:
        corner = other[(0,) * (other.ndim - 2)][:16, :128].astype(F32)
        value = value + jnp.minimum(jnp.max(jnp.abs(corner)), 0.0)
    return value


def line_gather(block):
    n, p = lax.axis_size("mx"), lax.axis_index("mx")
    up, down = [block], [block]
    for s in range(1, n):
        up.append(lax.ppermute(up[-1], "mx", [(i, i + 1) for i in range(s - 1, n - 1)]))
        down.append(lax.ppermute(down[-1], "mx", [(i, i - 1) for i in range(1, n - s + 1)]))
    slots = [block] + [jnp.where(p >= r, up[r], down[n - r]) for r in range(1, n)]
    return jnp.concatenate(slots, axis=0), (up[-2], down[-2])


def line_scatter(part):
    n = part.shape[0]
    up = down = None
    seen = []
    for s in range(1, n):
        send_up = part[s] if up is None else add(part[s], up).astype(BF16)
        send_down = part[n - s] if down is None else add(part[n - s], down).astype(BF16)
        up = lax.ppermute(send_up, "mx", [(i, i + 1) for i in range(s)])
        down = lax.ppermute(send_down, "mx", [(i, i - 1) for i in range(n - s, n)])
        seen.append((up, down))
    return add(part[0], up, down), seen[-2]


def rows_in_line_order(block):
    n, p = lax.axis_size("mx"), lax.axis_index("mx")
    both = jnp.stack([block, swap(block)])
    whole = lax.all_gather(both, "my", axis=1, tiled=True)
    whole = whole.reshape(2, n, whole.shape[1] // n, whole.shape[2])
    slots = [lax.dynamic_index_in_dim(whole, (p - r) % n, 1, False) for r in range(n)]
    return jnp.concatenate(slots, axis=0).reshape(-1, block.shape[1])


def scatter_rows(part):
    me = lax.axis_index("my")
    bit = 1
    while part.shape[1] > 1:
        pairs = part.reshape(2, part.shape[1] // 2, 2, *part.shape[2:])
        mine = (me // bit) % 2
        keep = jnp.where(mine == 0, pairs[:, :, 0], pairs[:, :, 1])
        send = jnp.where(mine == 0, pairs[:, :, 1], pairs[:, :, 0]).astype(BF16)
        got = lax.ppermute(send, "my", [(i, i ^ bit) for i in range(lax.axis_size("my"))])
        part = add(keep, got)
        bit *= 2
    return add(part[0, 0], swap(part[1, 0].astype(BF16))).astype(BF16)


def per_device(inputs, hidden_in, out_grad, up_weight, down_weight):
    n, p, dp = lax.axis_size("mx"), lax.axis_index("mx"), lax.axis_index("dp")
    n_my = lax.axis_size("my")
    total_tokens = out_grad.shape[0] * n_my * lax.axis_size("dp")
    grad_scale = 1.0 / jnp.sqrt(jnp.float32(total_tokens))
    rows, ff = hidden_in.shape
    width = inputs.shape[1]
    half = ff // 2
    chunks = 4
    w = half // chunks

    grad_rows = rows_in_line_order(out_grad)

    hidden = []
    for c in range(chunks):
        low, high = hidden_in[:, c * w:(c + 1) * w], hidden_in[:, half + c * w:half + (c + 1) * w]
        mine, other = jnp.where(dp == 0, low, high), jnp.where(dp == 0, high, low)
        hidden.append(jnp.concatenate([mine, swap(other)], axis=0).astype(F32))

    input_rows = rows_in_line_order(after(inputs.astype(F32), grad_rows).astype(BF16))

    down_grad = jnp.zeros(down_weight.shape, BF16)
    up_grad = jnp.zeros(up_weight.shape, BF16)
    inputs_part = None
    act_all, act_mid, down_own, down_got, up_own, up_got = [], [], [], [], [], []
    part_mid = ()

    def gather_act(c):
        gates = act_mid[c - 1] if c > 0 else ()
        act = after(gelu_value(hidden[c]), *gates).astype(BF16)
        whole, middle = line_gather(act)
        act_all.append(whole)
        act_mid.append(middle)

    gather_act(0)
    for c in range(chunks):
        own = (
            jnp.einsum("tf,td->fd", act_all[c], grad_rows, preferred_element_type=F32) * grad_scale
        ).astype(BF16)
        got = swap(own)
        down_own.append(own)
        down_got.append(got)
        down_grad = lax.dynamic_update_slice(down_grad, jnp.where(dp == 0, own, got), (c * w, 0))
        down_grad = lax.dynamic_update_slice(
            down_grad, jnp.where(dp == 0, got, own), (half + c * w, 0)
        )

        weight = lax.dynamic_slice_in_dim(down_weight, dp * half + c * w, w, 0)
        part = jnp.einsum("td,fd->tf", grad_rows, weight, preferred_element_type=F32)
        gates = part_mid
        if c == 0:
            gates += act_mid[0]
        if c > 0:
            gates += (down_own[c - 1],)
        if c > 1:
            gates += (down_got[c - 2],)
        part = after(part, *gates).astype(BF16).reshape(n, 2 * rows, w)
        act_grad, part_mid = line_scatter(part)
        gates = ()
        if c + 1 < chunks:
            gather_act(c + 1)
            gates += act_mid[c + 1]
        else:
            gates += (down_got[c],)
        if c > 1:
            gates += (up_got[c - 2],)
        pre_grad = after(act_grad * gelu_slope(hidden[c]), *gates).astype(BF16)
        pre_all, _ = line_gather(pre_grad)

        own = jnp.einsum("td,tf->df", input_rows, pre_all, preferred_element_type=F32) * grad_scale
        if c == chunks - 1:
            own = after(own, up_got[c - 1])
        own = own.astype(BF16)
        got = swap(own)
        up_own.append(own)
        up_got.append(got)
        up_grad = lax.dynamic_update_slice(up_grad, jnp.where(dp == 0, own, got), (0, c * w))
        up_grad = lax.dynamic_update_slice(
            up_grad, jnp.where(dp == 0, got, own), (0, half + c * w)
        )

        weight = lax.dynamic_slice_in_dim(up_weight, dp * half + c * w, w, 1)
        term = jnp.einsum("tf,df->td", pre_all, weight, preferred_element_type=F32)
        inputs_part = term if inputs_part is None else inputs_part + term
    inputs_part = after(inputs_part, up_own[-1])

    slots = inputs_part.reshape(n, 2, rows, width)
    blocks = [lax.dynamic_index_in_dim(slots, (p - q) % n, 0, False) for q in range(n)]
    part = jnp.concatenate(blocks, axis=1)
    inputs_grad = scatter_rows(part.reshape(2, n_my, -1, width))
    return inputs_grad, up_grad, down_grad


def solution(mesh):
    return jax.shard_map(
        per_device,
        mesh=mesh,
        in_specs=(
            P(("dp", "my"), "mx"),
            P(("dp", "mx"), "my"),
            P(("dp", "my"), "mx"),
            P("mx", "my"),
            P("my", "mx"),
        ),
        out_specs=(P(("dp", "my"), "mx"), P("mx", "my"), P("my", "mx")),
        check_vma=False,
    )
```

time: 1900 us -> 948 us (0.50)
  waiting for transfers between devices: 1720 us -> 357 us
  starting transfers between devices: 0.46 us -> 192 us
  other arithmetic: 10.5 us -> 168 us
  matrix products: 109 us -> 145 us
    psum x1 -> x0, waiting for transfers between devices: 830 us -> none  [per_device(): lax.psum(up_part.astype(jnp.bfloat16), 'dp').astype(jnp.float32)]
    reduce_scatter x2 -> x0, waiting for transfers between devices: 447 us -> none  [the longest x1 414 us: per_device(): lax.psum_scatter(jnp.einsum('td,fd->tf', row_block, down_weight, preferre...]
    all_gather x4 -> x2, waiting for transfers between devices: 444 us -> 0.01 us  [rows_in_line_order(): whole = lax.all_gather(both, 'my', axis=1, tiled=True)]
    ppermute x0 -> x89, waiting for transfers between devices: none -> 357 us  [the longest x24 163 us: line_gather(): lax.ppermute(down[-1], 'mx', [(i, i - 1) for i in range(1, n - s + 1)])]
    ppermute x0 -> x89, starting transfers between devices: none -> 192 us  [the longest x12 67.1 us: line_scatter(): up = lax.ppermute(send_up, 'mx', [(i, i + 1) for i in range(s)])]
    dynamic_update_slice x0 -> x14, other arithmetic: none -> 41.9 us  [the longest x4 15.1 us: per_device(): lax.dynamic_update_slice(down_grad, jnp.where(dp == 0, got, own), (half +...]
    select_n x0 -> x27, other arithmetic: none -> 39.2 us  [the longest x24 32.5 us: line_gather(): jnp.where(p >= r, up[r], down[n - r])]
    dot_general x4 -> x16, matrix products: 109 us -> 145 us  [the longest x4 56.4 us: per_device(): term = jnp.einsum('tf,df->td', pre_all, weight, preferred_element_type=F32)]
  transfers between devices with their start and end apart: 7 -> 91, of which waited for: 6 -> 29; matrix products, arithmetic and copies ran while one was open for 4% -> 30% of each run, Pallas kernels for 0% -> 0%
where the time goes in v1:
time: 948 us; the launch traced here: 936 us
  waiting for transfers between devices  357 us (38%)
  starting transfers between devices  192 us (20%)
  other arithmetic  168 us (18%)
  matrix products  145 us (15%)
  local copies, waits for them, and re-layouts  42.3 us (4%)
  between operations  32.3 us (3%)
    ppermute x24, waiting for transfers between devices, line_gather(): lax.ppermute(down[-1], 'mx', [(i, i - 1) for i in range(1, n - s + 1)])  163 us
    ppermute x15, waiting for transfers between devices, swap(): return lax.ppermute(block, 'dp', [(0, 1), (1, 0)])  139 us
    ppermute x12, starting transfers between devices, line_scatter(): up = lax.ppermute(send_up, 'mx', [(i, i + 1) for i in range(s)])  67.1 us
    ppermute x24, starting transfers between devices, line_gather(): lax.ppermute(up[-1], 'mx', [(i, i + 1) for i in range(s - 1, n - 1)])  59 us
    dot_general x4, matrix products, per_device(): term = jnp.einsum('tf,df->td', pre_all, weight, preferred_element_type=F32)  56.4 us
    select_n x24, other arithmetic, line_gather(): jnp.where(p >= r, up[r], down[n - r])  32.5 us
    ppermute x24, starting transfers between devices, line_gather(): lax.ppermute(down[-1], 'mx', [(i, i - 1) for i in range(1, n - s + 1)])  31.4 us
    dot_general x4, matrix products, per_device(): jnp.einsum('td,fd->tf', grad_rows, weight, preferred_element_type=F32)  31 us
  transfers between devices with their start and end apart: 91, of which 29 were waited for; matrix products, arithmetic and copies ran while one was open for 30% of the time, Pallas kernels for 0%

profile of v1, /device:TPU:0, one launch (start us, length us, event | category | flops | bytes accessed | tf_op | source)
XLA Modules:
  0.0 935.9 jit_solution(145456349212970517)
XLA Ops:
  10.2 17.8 %collective-permute-done = bf16[256,1536]{1,0:T(8,128)(2,1)S(1)} collective-permute-done((bf16[256,1536]{1,0:T(8,128)(2,1)}, bf16[256,1536]{1,0:T(8,128)(2,1)S(1)}, u32[]{:S(2)}, u32[]{:S(2)}) %collective-permute-start) | collective-permute-done | bytes 786464 | tf_op jit(solution)/shard_map/ppermute | solution.py:21
  35.3 8.6 collective-permute-done.1
  45.5 5.5 collective-permute-start.2
  51.0 12.9 %collective-permute-done.4 = bf16[512,768]{1,0:T(8,128)(2,1)S(1)} collective-permute-done((bf16[512,768]{1,0:T(8,128)(2,1)S(1)}, bf16[512,768]{1,0:T(8,128)(2,1)S(1)}, u32[]{:S(2)}, u32[]{:S(2)}) %collective-permute-start.4) | collective-permute-done | bytes 786464 | tf_op jit(solution)/shard_map/ppermute | solution.py:43
  67.1 15.7 %collective-permute-done.5 = bf16[512,768]{1,0:T(8,128)(2,1)S(1)} collective-permute-done((bf16[512,768]{1,0:T(8,128)(2,1)S(1)}, bf16[512,768]{1,0:T(8,128)(2,1)S(1)}, u32[]{:S(2)}, u32[]{:S(2)}) %collective-permute-start.5) | collective-permute-done | bytes 786464 | tf_op jit(solution)/shard_map/ppermute | solution.py:43
  88.2 5.5 collective-permute-start.13
  93.7 11.1 %collective-permute-done.15 = bf16[512,768]{1,0:T(8,128)(2,1)S(1)} collective-permute-done((bf16[512,768]{1,0:T(8,128)(2,1)S(1)}, bf16[512,768]{1,0:T(8,128)(2,1)S(1)}, u32[]{:S(2)}, u32[]{:S(2)}) %collective-permute-start.15) | collective-permute-done | bytes 786464 | tf_op jit(solution)/shard_map/ppermute | solution.py:43
  108.2 13.7 %collective-permute-done.16 = bf16[512,768]{1,0:T(8,128)(2,1)} collective-permute-done((bf16[512,768]{1,0:T(8,128)(2,1)S(1)}, bf16[512,768]{1,0:T(8,128)(2,1)}, u32[]{:S(2)}, u32[]{:S(2)}) %collective-permute-start.16) | collective-permute-done | bytes 786464 | tf_op jit(solution)/shard_map/ppermute | solution.py:43
  127.9 5.5 collective-permute-start.32
  134.6 14.4 %collective-permute-done.34 = bf16[512,768]{1,0:T(8,128)(2,1)} collective-permute-done((bf16[512,768]{1,0:T(8,128)(2,1)S(1)}, bf16[512,768]{1,0:T(8,128)(2,1)}, u32[]{:S(2)}, u32[]{:S(2)}) %collective-permute-start.34) | collective-permute-done | bytes 786464 | tf_op jit(solution)/shard_map/ppermute | solution.py:43
  155.9 10.0 %collective-permute-done.23 = bf16[512,768]{1,0:T(8,128)(2,1)} collective-permute-done((bf16[512,768]{1,0:T(8,128)(2,1)}, bf16[512,768]{1,0:T(8,128)(2,1)}, u32[]{:S(2)}, u32[]{:S(2)}) %collective-permute-start.23) | collective-permute-done | bytes 786464 | tf_op jit(solution)/shard_map/ppermute | solution.py:43
  169.3 13.5 %collective-permute-done.35 = bf16[512,768]{1,0:T(8,128)(2,1)} collective-permute-done((bf16[512,768]{1,0:T(8,128)(2,1)}, bf16[512,768]{1,0:T(8,128)(2,1)}, u32[]{:S(2)}, u32[]{:S(2)}) %collective-permute-start.35) | collective-permute-done | bytes 786464 | tf_op jit(solution)/shard_map/ppermute | solution.py:43
  203.2 13.2 %collective-permute-done.54 = bf16[512,768]{1,0:T(8,128)(2,1)S(1)} collective-permute-done((bf16[512,768]{1,0:T(8,128)(2,1)S(1)}, bf16[512,768]{1,0:T(8,128)(2,1)S(1)}, u32[]{:S(2)}, u32[]{:S(2)}) %collective-permute-start.54) | collective-permute-done | bytes 786464 | tf_op jit(solution)/shard_map/ppermute | solution.py:43
  221.5 11.7 %collective-permute-done.64 = bf16[512,768]{1,0:T(8,128)(2,1)S(1)} collective-permute-done((bf16[512,768]{1,0:T(8,128)(2,1)}, bf16[512,768]{1,0:T(8,128)(2,1)S(1)}, u32[]{:S(2)}, u32[]{:S(2)}) %collective-permute-start.64) | collective-permute-done | bytes 786464 | tf_op jit(solution)/shard_map/ppermute | solution.py:43
  234.2 11.1 %collective-permute-done.55 = bf16[512,768]{1,0:T(8,128)(2,1)S(1)} collective-permute-done((bf16[512,768]{1,0:T(8,128)(2,1)S(1)}, bf16[512,768]{1,0:T(8,128)(2,1)S(1)}, u32[]{:S(2)}, u32[]{:S(2)}) %collective-permute-start.55) | collective-permute-done | bytes 786464 | tf_op jit(solution)/shard_map/ppermute | solution.py:43
  254.1 6.7 collective-permute-done.73
  273.1 9.9 %multiply_convert_fusion.6 = bf16[768,1536]{1,0:T(8,128)(2,1)} fusion(bf16[2048,1536]{1,0:T(8,128)(2,1)} %bitcast.109, bf16[512,768]{1,0:T(8,128)(2,1)} %broadcast_select_fusion.8, bf16[512,768]{1,0:T(8,128)(2,1)S(1)} %copy-done.50, bf16[512,768]{1,0:T(8,128)(2,1)S(1)} %copy-done.51, bf16[512,768]{1,0:T(8,128)(2,1)} %copy-done.61), kind=kOutput, calls=%fused_computation.20 | convolution fusion | flops 4846780416 | bytes 11796480 | tf_op jit(solution)/shard_map/tf,td->fd/dot_general | solution.py:121
  284.5 7.0 add_convert_fusion.3
  294.5 6.4 multiply_convert_fusion.2
  306.3 5.3 collective-permute-start.7
  313.2 5.4 multiply_convert_fusion.5
  324.4 8.0 add_convert_fusion.2
  332.6 12.1 %collective-permute-start.25 = (bf16[512,768]{1,0:T(8,128)(2,1)S(1)}, bf16[512,768]{1,0:T(8,128)(2,1)S(1)}, u32[]{:S(2)}, u32[]{:S(2)}) collective-permute-start(bf16[512,768]{1,0:T(8,128)(2,1)S(1)} %get-tuple-element.41), channel_id=1, source_target_pairs={{0,4},{1,5},{2,6},{3,7},{16,20},{17,21},{18,22},{19,23}} | collective-permute-start | bytes 2359304 | tf_op jit(solution)/shard_map/ppermute | solution.py:55
  351.7 10.9 %collective-permute-done.25 = bf16[512,768]{1,0:T(8,128)(2,1)S(1)} collective-permute-done((bf16[512,768]{1,0:T(8,128)(2,1)S(1)}, bf16[512,768]{1,0:T(8,128)(2,1)S(1)}, u32[]{:S(2)}, u32[]{:S(2)}) %collective-permute-start.25) | collective-permute-done | bytes 786464 | tf_op jit(solution)/shard_map/ppermute | solution.py:55
  365.5 6.0 collective-permute-start.26
  384.6 5.5 collective-permute-start.17
  390.1 6.4 collective-permute-done.26
  404.0 5.4 collective-permute-start.27
  409.4 8.0 add_convert_fusion.1
  424.6 6.4 multiply_convert_fusion.3
  440.3 10.2 %collective-permute-start.46 = (bf16[512,768]{1,0:T(8,128)(2,1)}, bf16[512,768]{1,0:T(8,128)(2,1)}, u32[]{:S(2)}, u32[]{:S(2)}) collective-permute-start(bf16[512,768]{1,0:T(8,128)(2,1)} %get-tuple-element.35), channel_id=1, source_target_pairs={{0,4},{4,8},{1,5},{5,9},{2,6},{6,10},{3,7},{7,11},{16,20},{20,24},... | collective-permute-start | bytes 2359304 | tf_op jit(solution)/shard_map/ppermute | solution.py:55
  457.4 8.0 dynamic_update_slice.56
  469.8 5.5 collective-permute-start.36
  482.0 8.0 add_convert_fusion
  491.9 5.7 collective-permute-start.67
  497.6 5.0 collective-permute-done.20
  508.9 7.3 collective-permute-done.38
  521.9 5.5 collective-permute-start.68
  538.2 7.2 multiply_convert_fusion.4
  546.5 7.7 multiply_convert_fusion.1
  562.7 4.9 collective-permute-start.47
  567.6 32.1 %collective-permute-done.57 = bf16[1536,768]{1,0:T(8,128)(2,1)S(1)} collective-permute-done((bf16[1536,768]{1,0:T(8,128)(2,1)S(1)}, bf16[1536,768]{1,0:T(8,128)(2,1)S(1)}, u32[]{:S(2)}, u32[]{:S(2)}) %collective-permute-start.57) | collective-permute-done | bytes 2359328 | tf_op jit(solution)/shard_map/ppermute | solution.py:21
  607.6 5.6 collective-permute-start.69
  613.3 5.7 collective-permute-done.50
  625.0 25.3 %collective-permute-done.76 = bf16[1536,768]{1,0:T(8,128)(2,1)} collective-permute-done((bf16[1536,768]{1,0:T(8,128)(2,1)}, bf16[1536,768]{1,0:T(8,128)(2,1)}, u32[]{:S(2)}, u32[]{:S(2)}) %collective-permute-start.76) | collective-permute-done | bytes 2359328 | tf_op jit(solution)/shard_map/ppermute | solution.py:21
  650.3 4.9 collective-permute-start.58
  666.5 4.6 collective-permute-start.77
  673.1 15.6 %collective-permute-done.88 = bf16[768,1536]{1,0:T(8,128)(2,1)} collective-permute-done((bf16[768,1536]{1,0:T(8,128)(2,1)}, bf16[768,1536]{1,0:T(8,128)(2,1)}, u32[]{:S(2)}, u32[]{:S(2)}) %collective-permute-start.88) | collective-permute-done | bytes 2359328 | tf_op jit(solution)/shard_map/ppermute | solution.py:21
  700.5 11.6 %fusion.45 = f32[2048,1536]{1,0:T(8,128)} fusion(bf16[1536,6144]{1,0:T(8,128)(2,1)} %param.8, s32[]{:T(128)S(6)} %select_n.359, bf16[512,768]{1,0:T(8,128)(2,1)S(1)} %copy-done.46, bf16[512,768]{1,0:T(8,128)(2,1)S(1)} %copy-done.38, bf16[512,768]{1,0:T(8,128)(2,1)S(1)} %copy-done.40, bf16[512,768]{1,0:T(8,128)(2,1)} %fusion.66), kind=kOutput, calls=%fused_computation.105 | convolution fusion | flops 4844421120 | bytes 18087940 | tf_op jit(solution)/shard_map/tf,df->td/dot_general | solution.py:166
  712.1 6.7 collective-permute-done.79
  721.1 9.8 %collective-permute-done.61 = bf16[512,768]{1,0:T(8,128)(2,1)S(1)} collective-permute-done((bf16[512,768]{1,0:T(8,128)(2,1)S(1)}, bf16[512,768]{1,0:T(8,128)(2,1)S(1)}, u32[]{:S(2)}, u32[]{:S(2)}) %collective-permute-start.61) | collective-permute-done | bytes 786464 | tf_op jit(solution)/shard_map/ppermute | solution.py:43
  732.3 6.4 multiply_convert_fusion
  739.9 11.6 %fusion.42 = f32[2048,1536]{1,0:T(8,128)} fusion(bf16[1536,6144]{1,0:T(8,128)(2,1)} %param.8, s32[]{:T(128)S(6)} %select_n.371, bf16[512,768]{1,0:T(8,128)(2,1)S(1)} %copy-done.48, bf16[512,768]{1,0:T(8,128)(2,1)S(1)} %copy-done.42, bf16[512,768]{1,0:T(8,128)(2,1)S(1)} %copy-done.44, bf16[512,768]{1,0:T(8,128)(2,1)} %fusion.79), kind=kOutput, calls=%fused_computation.102 | convolution fusion | flops 4844421120 | bytes 18087940 | tf_op jit(solution)/shard_map/tf,df->td/dot_general | solution.py:166
  751.8 12.3 %fusion.39 = f32[2048,1536]{1,0:T(8,128)} fusion(bf16[1536,6144]{1,0:T(8,128)(2,1)} %param.8, s32[]{:T(128)S(6)} %select_n.380, bf16[512,768]{1,0:T(8,128)(2,1)S(1)} %broadcast_select_fusion.5, bf16[512,768]{1,0:T(8,128)(2,1)S(1)} %broadcast_select_fusion.13, bf16[512,768]{1,0:T(8,128)(2,1)S(1)} %broadcast_select_fusion.21, bf16[512,768]{1,0:T(8,128)(2,1)} %fusion.93), kind=kOutput, calls=%fused_computation.99 | convolution fusion | flops 4844421120 | bytes 18087940 | tf_op jit(solution)/shard_map/tf,df->td/dot_general | solution.py:166
  764.1 6.4 collective-permute-done.83
  773.2 7.9 add_convert_fusion.4
  783.8 20.9 %add_add_fusion = f32[2048,1536]{1,0:T(8,128)} fusion(f32[2048,1536]{1,0:T(8,128)} %fusion.39, f32[2048,1536]{1,0:T(8,128)} %fusion.45, f32[2048,1536]{1,0:T(8,128)} %fusion.42, f32[]{:T(128)S(6)} %min.105, bf16[1536,6144]{1,0:T(8,128)(2,1)} %param.8, s32[]{:T(128)S(6)} %select_n.389, bf16[512,768]{1,0:T(8,128)(2,1)S(1)} %broadcast_select_fusion.2, ...), kind=kOutput, calls=%fused_computation.1 | convolution fusion | flops 4857004032 | bytes 55836680 | tf_op jit(solution)/shard_map/tf,df->td/dot_general | solution.py:166
  804.7 10.1 %dynamic-slice_bitcast_fusion.3 = (f32[2,256,1536]{2,1,0:T(8,128)}, f32[2,256,1536]{2,1,0:T(8,128)}, f32[2,256,1536]{2,1,0:T(8,128)}, f32[2,256,1536]{2,1,0:T(8,128)}) fusion(f32[4,2,256,1536]{3,2,1,0:T(8,128)} %bitcast.106, s32[]{:T(128)S(6)} %select_n.352, s32[]{:T(128)S(6)} %select_n.358, s32[]{:T(128)S(6)} %select_n.356, s32[]{:T(128)S(6)} %select_n.354), kind=kLoop, calls=%fused_computation.61 | loop fusion | bytes 25165840 | tf_op jit(solution)/shard_map/jit(dynamic_index_in_dim)/squeeze | solution.py:171
  814.8 5.6 pad_maximum_fusion
  828.8 7.1 dynamic_update_slice.48
  841.4 6.2 fusion.2
  861.8 26.9 %collective-permute-done.85 = bf16[2,1,256,1536]{3,2,0,1:T(8,128)(2,1)S(1)} collective-permute-done((bf16[2,1,256,1536]{3,2,0,1:T(8,128)(2,1)S(1)}, bf16[2,1,256,1536]{3,2,0,1:T(8,128)(2,1)S(1)}, u32[]{:S(2)}, u32[]{:S(2)}) %collective-permute-start.85) | collective-permute-done | bytes 1572896 | tf_op jit(solution)/shard_map/ppermute | solution.py:78
  890.0 21.6 %collective-permute-done.87 = bf16[1536,768]{1,0:T(8,128)(2,1)S(1)} collective-permute-done((bf16[1536,768]{1,0:T(8,128)(2,1)S(1)}, bf16[1536,768]{1,0:T(8,128)(2,1)S(1)}, u32[]{:S(2)}, u32[]{:S(2)}) %collective-permute-start.87) | collective-permute-done | bytes 2359328 | tf_op jit(solution)/shard_map/ppermute | solution.py:21
  915.6 12.0 %collective-permute-done.86 = bf16[256,1536]{1,0:T(8,128)(2,1)S(1)} collective-permute-done((bf16[256,1536]{1,0:T(8,128)(2,1)S(1)}, bf16[256,1536]{1,0:T(8,128)(2,1)S(1)}, u32[]{:S(2)}, u32[]{:S(2)}) %collective-permute-start.86) | collective-permute-done | bytes 786464 | tf_op jit(solution)/shard_map/ppermute | solution.py:21
  (400 shorter events, 272.4 us)
Async XLA Ops:
  7.2 256.8 %all-gather.3.cloned.1.call-start = ((), (), s32[]{:S(2)}) async-start(), calls=%async_computation | async-start | bytes 7864320 | tf_op jit(solution)/shard_map/all_gather | solution.py:64
  7.2 20.8 %collective-permute-start = (bf16[256,1536]{1,0:T(8,128)(2,1)}, bf16[256,1536]{1,0:T(8,128)(2,1)S(1)}, u32[]{:S(2)}, u32[]{:S(2)}) collective-permute-start(bf16[256,1536]{1,0:T(8,128)(2,1)} %param.7), channel_id=1, source_target_pairs={{0,16},{16,0},{1,17},{17,1},{2,18},{18,2},{3,19},{19,3},{4,20},{20... | collective-permute-start | bytes 2359304 | tf_op jit(solution)/shard_map/ppermute | solution.py:21
  30.4 503.1 %all-gather.5.cloned.1.call-start = ((), (), s32[]{:S(2)}) async-start(), calls=%async_computation.1 | async-start | bytes 7864320 | tf_op jit(solution)/shard_map/all_gather | solution.py:64
  126.6 22.5 %collective-permute-start.34 = (bf16[512,768]{1,0:T(8,128)(2,1)S(1)}, bf16[512,768]{1,0:T(8,128)(2,1)}, u32[]{:S(2)}, u32[]{:S(2)}) collective-permute-start(bf16[512,768]{1,0:T(8,128)(2,1)S(1)} %fusion.83), channel_id=1, source_target_pairs={{4,0},{8,4},{12,8},{5,1},{9,5},{13,9},{6,2},{10,6},{14,10},{7,3},{... | collective-permute-start | bytes 2359304 | tf_op jit(solution)/shard_map/ppermute | solution.py:43
  127.9 22.5 %collective-permute-start.32 = (bf16[512,768]{1,0:T(8,128)(2,1)S(1)}, bf16[512,768]{1,0:T(8,128)(2,1)}, u32[]{:S(2)}, u32[]{:S(2)}) collective-permute-start(bf16[512,768]{1,0:T(8,128)(2,1)S(1)} %fusion.83), channel_id=1, source_target_pairs={{0,4},{4,8},{8,12},{1,5},{5,9},{9,13},{2,6},{6,10},{10,14},{3,7},{... | collective-permute-start | bytes 2359304 | tf_op jit(solution)/shard_map/ppermute | solution.py:42
  133.3 32.6 %collective-permute-start.23 = (bf16[512,768]{1,0:T(8,128)(2,1)}, bf16[512,768]{1,0:T(8,128)(2,1)}, u32[]{:S(2)}, u32[]{:S(2)}) collective-permute-start(bf16[512,768]{1,0:T(8,128)(2,1)} %copy-done.30), channel_id=1, source_target_pairs={{4,0},{5,1},{6,2},{7,3},{20,16},{21,17},{22,18},{23,19}} | collective-permute-start | bytes 2359304 | tf_op jit(solution)/shard_map/ppermute | solution.py:43
  149.0 33.7 %collective-permute-start.35 = (bf16[512,768]{1,0:T(8,128)(2,1)}, bf16[512,768]{1,0:T(8,128)(2,1)}, u32[]{:S(2)}, u32[]{:S(2)}) collective-permute-start(bf16[512,768]{1,0:T(8,128)(2,1)} %collective-permute-done.34), channel_id=1, source_target_pairs={{4,0},{8,4},{5,1},{9,5},{6,2},{10,6},{7,3},{11,7},{20,16},{24,20},... | collective-permute-start | bytes 2359304 | tf_op jit(solution)/shard_map/ppermute | solution.py:43
  150.3 35.9 %collective-permute-start.33 = (bf16[512,768]{1,0:T(8,128)(2,1)}, bf16[512,768]{1,0:T(8,128)(2,1)}, u32[]{:S(2)}, u32[]{:S(2)}) collective-permute-start(bf16[512,768]{1,0:T(8,128)(2,1)} %collective-permute-done.32), channel_id=1, source_target_pairs={{4,8},{8,12},{5,9},{9,13},{6,10},{10,14},{7,11},{11,15},{20,24},{2... | collective-permute-start | bytes 2359304 | tf_op jit(solution)/shard_map/ppermute | solution.py:42
  151.9 36.3 %collective-permute-start.51 = (bf16[256,768]{1,0:T(8,128)(2,1)}, bf16[256,768]{1,0:T(8,128)(2,1)S(1)}, u32[]{:S(2)}, u32[]{:S(2)}) collective-permute-start(bf16[256,768]{1,0:T(8,128)(2,1)} %get-tuple-element.29), channel_id=1, source_target_pairs={{0,16},{16,0},{1,17},{17,1},{2,18},{18,2},{3,19},{19,3},{4,20},{20... | collective-permute-start | bytes 1179656 | tf_op jit(solution)/shard_map/ppermute | solution.py:21
  152.2 37.9 %collective-permute-start.24 = (bf16[512,768]{1,0:T(8,128)(2,1)S(1)}, bf16[512,768]{1,0:T(8,128)(2,1)}, u32[]{:S(2)}, u32[]{:S(2)}) collective-permute-start(bf16[512,768]{1,0:T(8,128)(2,1)S(1)} %collective-permute-done.3), channel_id=1, source_target_pairs={{8,12},{9,13},{10,14},{11,15},{24,28},{25,29},{26,30},{27,31}} | collective-permute-start | bytes 2359304 | tf_op jit(solution)/shard_map/ppermute | solution.py:42
  168.0 32.3 %collective-permute-start.42 = (bf16[512,768]{1,0:T(8,128)(2,1)}, bf16[512,768]{1,0:T(8,128)(2,1)}, u32[]{:S(2)}, u32[]{:S(2)}) collective-permute-start(bf16[512,768]{1,0:T(8,128)(2,1)} %collective-permute-done.16), channel_id=1, source_target_pairs={{4,0},{5,1},{6,2},{7,3},{20,16},{21,17},{22,18},{23,19}} | collective-permute-start | bytes 2359304 | tf_op jit(solution)/shard_map/ppermute | solution.py:43
  182.8 34.9 %collective-permute-start.43 = (bf16[512,768]{1,0:T(8,128)(2,1)}, bf16[512,768]{1,0:T(8,128)(2,1)}, u32[]{:S(2)}, u32[]{:S(2)}) collective-permute-start(bf16[512,768]{1,0:T(8,128)(2,1)} %collective-permute-done.14), channel_id=1, source_target_pairs={{8,12},{9,13},{10,14},{11,15},{24,28},{25,29},{26,30},{27,31}} | collective-permute-start | bytes 2359304 | tf_op jit(solution)/shard_map/ppermute | solution.py:42
  188.7 27.6 %collective-permute-start.54 = (bf16[512,768]{1,0:T(8,128)(2,1)S(1)}, bf16[512,768]{1,0:T(8,128)(2,1)S(1)}, u32[]{:S(2)}, u32[]{:S(2)}) collective-permute-start(bf16[512,768]{1,0:T(8,128)(2,1)S(1)} %fusion.97), channel_id=1, source_target_pairs={{4,0},{8,4},{12,8},{5,1},{9,5},{13,9},{6,2},{10,6},{14,10},{7,3},{... | collective-permute-start | bytes 2359304 | tf_op jit(solution)/shard_map/ppermute | solution.py:43
  192.3 26.4 %collective-permute-start.52 = (bf16[512,768]{1,0:T(8,128)(2,1)S(1)}, bf16[512,768]{1,0:T(8,128)(2,1)S(1)}, u32[]{:S(2)}, u32[]{:S(2)}) collective-permute-start(bf16[512,768]{1,0:T(8,128)(2,1)S(1)} %fusion.97), channel_id=1, source_target_pairs={{0,4},{4,8},{8,12},{1,5},{5,9},{9,13},{2,6},{6,10},{10,14},{3,7},{... | collective-permute-start | bytes 2359304 | tf_op jit(solution)/shard_map/ppermute | solution.py:42
  199.0 34.2 %collective-permute-start.64 = (bf16[512,768]{1,0:T(8,128)(2,1)}, bf16[512,768]{1,0:T(8,128)(2,1)S(1)}, u32[]{:S(2)}, u32[]{:S(2)}) collective-permute-start(bf16[512,768]{1,0:T(8,128)(2,1)} %collective-permute-done.35), channel_id=1, source_target_pairs={{4,0},{5,1},{6,2},{7,3},{20,16},{21,17},{22,18},{23,19}} | collective-permute-start | bytes 2359304 | tf_op jit(solution)/shard_map/ppermute | solution.py:43
  202.5 44.2 %collective-permute-start.65 = (bf16[512,768]{1,0:T(8,128)(2,1)}, bf16[512,768]{1,0:T(8,128)(2,1)S(1)}, u32[]{:S(2)}, u32[]{:S(2)}) collective-permute-start(bf16[512,768]{1,0:T(8,128)(2,1)} %collective-permute-done.33), channel_id=1, source_target_pairs={{8,12},{9,13},{10,14},{11,15},{24,28},{25,29},{26,30},{27,31}} | collective-permute-start | bytes 2359304 | tf_op jit(solution)/shard_map/ppermute | solution.py:42
  216.4 28.9 %collective-permute-start.55 = (bf16[512,768]{1,0:T(8,128)(2,1)S(1)}, bf16[512,768]{1,0:T(8,128)(2,1)S(1)}, u32[]{:S(2)}, u32[]{:S(2)}) collective-permute-start(bf16[512,768]{1,0:T(8,128)(2,1)S(1)} %collective-permute-done.54), channel_id=1, source_target_pairs={{4,0},{8,4},{5,1},{9,5},{6,2},{10,6},{7,3},{11,7},{20,16},{24,20},... | collective-permute-start | bytes 2359304 | tf_op jit(solution)/shard_map/ppermute | solution.py:43
  218.6 30.2 %collective-permute-start.53 = (bf16[512,768]{1,0:T(8,128)(2,1)S(1)}, bf16[512,768]{1,0:T(8,128)(2,1)S(1)}, u32[]{:S(2)}, u32[]{:S(2)}) collective-permute-start(bf16[512,768]{1,0:T(8,128)(2,1)S(1)} %collective-permute-done.52), channel_id=1, source_target_pairs={{4,8},{8,12},{5,9},{9,13},{6,10},{10,14},{7,11},{11,15},{20,24},{2... | collective-permute-start | bytes 2359304 | tf_op jit(solution)/shard_map/ppermute | solution.py:42
  273.0 99.8 %collective-permute-start.56 = (bf16[256,1536]{1,0:T(8,128)(2,1)}, bf16[256,1536]{1,0:T(8,128)(2,1)}, u32[]{:S(2)}, u32[]{:S(2)}) collective-permute-start(bf16[256,1536]{1,0:T(8,128)(2,1)} %add_convert_fusion.7), channel_id=1, source_target_pairs={{0,16},{16,0},{1,17},{17,1},{2,18},{18,2},{3,19},{19,3},{4,20},{20... | collective-permute-start | bytes 2359304 | tf_op jit(solution)/shard_map/ppermute | solution.py:21
  283.0 94.2 %collective-permute-start.44 = (bf16[768,1536]{1,0:T(8,128)(2,1)}, bf16[768,1536]{1,0:T(8,128)(2,1)}, u32[]{:S(2)}, u32[]{:S(2)}) collective-permute-start(bf16[768,1536]{1,0:T(8,128)(2,1)} %multiply_convert_fusion.6), channel_id=1, source_target_pairs={{0,16},{16,0},{1,17},{17,1},{2,18},{18,2},{3,19},{19,3},{4,20},{20... | collective-permute-start | bytes 7077896 | tf_op jit(solution)/shard_map/ppermute | solution.py:21
  332.6 30.1 %collective-permute-start.25 = (bf16[512,768]{1,0:T(8,128)(2,1)S(1)}, bf16[512,768]{1,0:T(8,128)(2,1)S(1)}, u32[]{:S(2)}, u32[]{:S(2)}) collective-permute-start(bf16[512,768]{1,0:T(8,128)(2,1)S(1)} %get-tuple-element.41), channel_id=1, source_target_pairs={{0,4},{1,5},{2,6},{3,7},{16,20},{17,21},{18,22},{19,23}} | collective-permute-start | bytes 2359304 | tf_op jit(solution)/shard_map/ppermute | solution.py:55
  349.4 30.7 %collective-permute-start.8 = (bf16[512,768]{1,0:T(8,128)(2,1)}, bf16[512,768]{1,0:T(8,128)(2,1)}, u32[]{:S(2)}, u32[]{:S(2)}) collective-permute-start(bf16[512,768]{1,0:T(8,128)(2,1)} %get-tuple-element.31), channel_id=1, source_target_pairs={{0,4},{4,8},{8,12},{1,5},{5,9},{9,13},{2,6},{6,10},{10,14},{3,7},{... | collective-permute-start | bytes 2359304 | tf_op jit(solution)/shard_map/ppermute | solution.py:55
  365.5 30.9 %collective-permute-start.26 = (bf16[512,768]{1,0:T(8,128)(2,1)}, bf16[512,768]{1,0:T(8,128)(2,1)}, u32[]{:S(2)}, u32[]{:S(2)}) collective-permute-start(bf16[512,768]{1,0:T(8,128)(2,1)} %get-tuple-element.39), channel_id=1, source_target_pairs={{0,4},{4,8},{1,5},{5,9},{2,6},{6,10},{3,7},{7,11},{16,20},{20,24},... | collective-permute-start | bytes 2359304 | tf_op jit(solution)/shard_map/ppermute | solution.py:55
  372.9 25.5 %collective-permute-start.29 = (bf16[512,768]{1,0:T(8,128)(2,1)}, bf16[512,768]{1,0:T(8,128)(2,1)}, u32[]{:S(2)}, u32[]{:S(2)}) collective-permute-start(bf16[512,768]{1,0:T(8,128)(2,1)} %get-tuple-element.40), channel_id=1, source_target_pairs={{8,4},{12,8},{9,5},{13,9},{10,6},{14,10},{11,7},{15,11},{24,20},{2... | collective-permute-start | bytes 2359304 | tf_op jit(solution)/shard_map/ppermute | solution.py:56
  377.2 63.1 %collective-permute-start.66 = (bf16[768,1536]{1,0:T(8,128)(2,1)S(1)}, bf16[768,1536]{1,0:T(8,128)(2,1)}, u32[]{:S(2)}, u32[]{:S(2)}) collective-permute-start(bf16[768,1536]{1,0:T(8,128)(2,1)S(1)} %multiply_convert_fusion.5), channel_id=1, source_target_pairs={{0,16},{16,0},{1,17},{17,1},{2,18},{18,2},{3,19},{19,3},{4,20},{20... | collective-permute-start | bytes 7077896 | tf_op jit(solution)/shard_map/ppermute | solution.py:21
  383.3 39.5 %collective-permute-start.18 = (bf16[512,768]{1,0:T(8,128)(2,1)}, bf16[512,768]{1,0:T(8,128)(2,1)}, u32[]{:S(2)}, u32[]{:S(2)}) collective-permute-start(bf16[512,768]{1,0:T(8,128)(2,1)} %fusion.66), channel_id=1, source_target_pairs={{4,0},{8,4},{12,8},{5,1},{9,5},{13,9},{6,2},{10,6},{14,10},{7,3},{... | collective-permute-start | bytes 2359304 | tf_op jit(solution)/shard_map/ppermute | solution.py:43
  384.6 48.3 %collective-permute-start.17 = (bf16[512,768]{1,0:T(8,128)(2,1)}, bf16[512,768]{1,0:T(8,128)(2,1)}, u32[]{:S(2)}, u32[]{:S(2)}) collective-permute-start(bf16[512,768]{1,0:T(8,128)(2,1)} %fusion.66), channel_id=1, source_target_pairs={{0,4},{4,8},{8,12},{1,5},{5,9},{9,13},{2,6},{6,10},{10,14},{3,7},{... | collective-permute-start | bytes 2359304 | tf_op jit(solution)/shard_map/ppermute | solution.py:42
  404.0 46.5 %collective-permute-start.27 = (bf16[512,768]{1,0:T(8,128)(2,1)}, bf16[512,768]{1,0:T(8,128)(2,1)}, u32[]{:S(2)}, u32[]{:S(2)}) collective-permute-start(bf16[512,768]{1,0:T(8,128)(2,1)} %get-tuple-element.21), channel_id=1, source_target_pairs={{0,4},{4,8},{8,12},{1,5},{5,9},{9,13},{2,6},{6,10},{10,14},{3,7},{... | collective-permute-start | bytes 2359304 | tf_op jit(solution)/shard_map/ppermute | solution.py:55
  432.9 32.4 %collective-permute-start.30 = (bf16[512,768]{1,0:T(8,128)(2,1)}, bf16[512,768]{1,0:T(8,128)(2,1)}, u32[]{:S(2)}, u32[]{:S(2)}) collective-permute-start(bf16[512,768]{1,0:T(8,128)(2,1)} %get-tuple-element.22), channel_id=1, source_target_pairs={{4,0},{8,4},{12,8},{5,1},{9,5},{13,9},{6,2},{10,6},{14,10},{7,3},{... | collective-permute-start | bytes 2359304 | tf_op jit(solution)/shard_map/ppermute | solution.py:56
  434.2 35.5 %collective-permute-start.19 = (bf16[512,768]{1,0:T(8,128)(2,1)}, bf16[512,768]{1,0:T(8,128)(2,1)}, u32[]{:S(2)}, u32[]{:S(2)}) collective-permute-start(bf16[512,768]{1,0:T(8,128)(2,1)} %collective-permute-done.18), channel_id=1, source_target_pairs={{4,0},{8,4},{5,1},{9,5},{6,2},{10,6},{7,3},{11,7},{20,16},{24,20},... | collective-permute-start | bytes 2359304 | tf_op jit(solution)/shard_map/ppermute | solution.py:43
  435.6 39.7 %collective-permute-start.21 = (bf16[512,768]{1,0:T(8,128)(2,1)}, bf16[512,768]{1,0:T(8,128)(2,1)}, u32[]{:S(2)}, u32[]{:S(2)}) collective-permute-start(bf16[512,768]{1,0:T(8,128)(2,1)} %collective-permute-done.17), channel_id=1, source_target_pairs={{4,8},{8,12},{5,9},{9,13},{6,10},{10,14},{7,11},{11,15},{20,24},{2... | collective-permute-start | bytes 2359304 | tf_op jit(solution)/shard_map/ppermute | solution.py:42
  440.3 36.2 %collective-permute-start.46 = (bf16[512,768]{1,0:T(8,128)(2,1)}, bf16[512,768]{1,0:T(8,128)(2,1)}, u32[]{:S(2)}, u32[]{:S(2)}) collective-permute-start(bf16[512,768]{1,0:T(8,128)(2,1)} %get-tuple-element.35), channel_id=1, source_target_pairs={{0,4},{4,8},{1,5},{5,9},{2,6},{6,10},{3,7},{7,11},{16,20},{20,24},... | collective-permute-start | bytes 2359304 | tf_op jit(solution)/shard_map/ppermute | solution.py:55
  450.5 29.5 %collective-permute-start.49 = (bf16[512,768]{1,0:T(8,128)(2,1)}, bf16[512,768]{1,0:T(8,128)(2,1)}, u32[]{:S(2)}, u32[]{:S(2)}) collective-permute-start(bf16[512,768]{1,0:T(8,128)(2,1)} %get-tuple-element.36), channel_id=1, source_target_pairs={{8,4},{12,8},{9,5},{13,9},{10,6},{14,10},{11,7},{15,11},{24,20},{2... | collective-permute-start | bytes 2359304 | tf_op jit(solution)/shard_map/ppermute | solution.py:56
  468.5 22.1 %collective-permute-start.37 = (bf16[512,768]{1,0:T(8,128)(2,1)}, bf16[512,768]{1,0:T(8,128)(2,1)}, u32[]{:S(2)}, u32[]{:S(2)}) collective-permute-start(bf16[512,768]{1,0:T(8,128)(2,1)} %fusion.79), channel_id=1, source_target_pairs={{4,0},{8,4},{12,8},{5,1},{9,5},{13,9},{6,2},{10,6},{14,10},{7,3},{... | collective-permute-start | bytes 2359304 | tf_op jit(solution)/shard_map/ppermute | solution.py:43
  469.8 33.6 %collective-permute-start.36 = (bf16[512,768]{1,0:T(8,128)(2,1)}, bf16[512,768]{1,0:T(8,128)(2,1)}, u32[]{:S(2)}, u32[]{:S(2)}) collective-permute-start(bf16[512,768]{1,0:T(8,128)(2,1)} %fusion.79), channel_id=1, source_target_pairs={{0,4},{4,8},{8,12},{1,5},{5,9},{9,13},{2,6},{6,10},{10,14},{3,7},{... | collective-permute-start | bytes 2359304 | tf_op jit(solution)/shard_map/ppermute | solution.py:42
  475.2 27.4 %collective-permute-start.20 = (bf16[512,768]{1,0:T(8,128)(2,1)}, bf16[512,768]{1,0:T(8,128)(2,1)S(1)}, u32[]{:S(2)}, u32[]{:S(2)}) collective-permute-start(bf16[512,768]{1,0:T(8,128)(2,1)} %collective-permute-done.19), channel_id=1, source_target_pairs={{4,0},{5,1},{6,2},{7,3},{20,16},{21,17},{22,18},{23,19}} | collective-permute-start | bytes 2359304 | tf_op jit(solution)/shard_map/ppermute | solution.py:43
  476.5 31.4 %collective-permute-start.22 = (bf16[512,768]{1,0:T(8,128)(2,1)}, bf16[512,768]{1,0:T(8,128)(2,1)}, u32[]{:S(2)}, u32[]{:S(2)}) collective-permute-start(bf16[512,768]{1,0:T(8,128)(2,1)} %collective-permute-done.21), channel_id=1, source_target_pairs={{8,12},{9,13},{10,14},{11,15},{24,28},{25,29},{26,30},{27,31}} | collective-permute-start | bytes 2359304 | tf_op jit(solution)/shard_map/ppermute | solution.py:42
  490.5 25.7 %collective-permute-start.38 = (bf16[512,768]{1,0:T(8,128)(2,1)}, bf16[512,768]{1,0:T(8,128)(2,1)S(1)}, u32[]{:S(2)}, u32[]{:S(2)}) collective-permute-start(bf16[512,768]{1,0:T(8,128)(2,1)} %collective-permute-done.37), channel_id=1, source_target_pairs={{4,0},{8,4},{5,1},{9,5},{6,2},{10,6},{7,3},{11,7},{20,16},{24,20},... | collective-permute-start | bytes 2359304 | tf_op jit(solution)/shard_map/ppermute | solution.py:43
  491.9 28.4 %collective-permute-start.67 = (bf16[512,768]{1,0:T(8,128)(2,1)S(1)}, bf16[512,768]{1,0:T(8,128)(2,1)S(1)}, u32[]{:S(2)}, u32[]{:S(2)}) collective-permute-start(bf16[512,768]{1,0:T(8,128)(2,1)S(1)} %get-tuple-element.19), channel_id=1, source_target_pairs={{0,4},{1,5},{2,6},{3,7},{16,20},{17,21},{18,22},{19,23}} | collective-permute-start | bytes 2359304 | tf_op jit(solution)/shard_map/ppermute | solution.py:55
  507.9 115.7 %collective-permute-start.75 = (bf16[768,1536]{1,0:T(8,128)(2,1)}, bf16[768,1536]{1,0:T(8,128)(2,1)}, u32[]{:S(2)}, u32[]{:S(2)}) collective-permute-start(bf16[768,1536]{1,0:T(8,128)(2,1)} %multiply_convert_fusion.2), channel_id=1, source_target_pairs={{0,16},{16,0},{1,17},{17,1},{2,18},{18,2},{3,19},{19,3},{4,20},{20... | collective-permute-start | bytes 7077896 | tf_op jit(solution)/shard_map/ppermute | solution.py:21
  521.9 39.9 %collective-permute-start.68 = (bf16[512,768]{1,0:T(8,128)(2,1)}, bf16[512,768]{1,0:T(8,128)(2,1)}, u32[]{:S(2)}, u32[]{:S(2)}) collective-permute-start(bf16[512,768]{1,0:T(8,128)(2,1)} %get-tuple-element.17), channel_id=1, source_target_pairs={{0,4},{4,8},{1,5},{5,9},{2,6},{6,10},{3,7},{7,11},{16,20},{20,24},... | collective-permute-start | bytes 2359304 | tf_op jit(solution)/shard_map/ppermute | solution.py:55
  527.4 35.3 %collective-permute-start.71 = (bf16[512,768]{1,0:T(8,128)(2,1)}, bf16[512,768]{1,0:T(8,128)(2,1)}, u32[]{:S(2)}, u32[]{:S(2)}) collective-permute-start(bf16[512,768]{1,0:T(8,128)(2,1)} %get-tuple-element.18), channel_id=1, source_target_pairs={{8,4},{12,8},{9,5},{13,9},{10,6},{14,10},{11,7},{15,11},{24,20},{2... | collective-permute-start | bytes 2359304 | tf_op jit(solution)/shard_map/ppermute | solution.py:56
  545.4 54.2 %collective-permute-start.57 = (bf16[1536,768]{1,0:T(8,128)(2,1)S(1)}, bf16[1536,768]{1,0:T(8,128)(2,1)S(1)}, u32[]{:S(2)}, u32[]{:S(2)}) collective-permute-start(bf16[1536,768]{1,0:T(8,128)(2,1)S(1)} %multiply_convert_fusion.4), channel_id=1, source_target_pairs={{0,16},{16,0},{1,17},{17,1},{2,18},{18,2},{3,19},{19,3},{4,20},{20... | collective-permute-start | bytes 7077896 | tf_op jit(solution)/shard_map/ppermute | solution.py:21
  554.1 96.2 %collective-permute-start.76 = (bf16[1536,768]{1,0:T(8,128)(2,1)}, bf16[1536,768]{1,0:T(8,128)(2,1)}, u32[]{:S(2)}, u32[]{:S(2)}) collective-permute-start(bf16[1536,768]{1,0:T(8,128)(2,1)} %multiply_convert_fusion.1), channel_id=1, source_target_pairs={{0,16},{16,0},{1,17},{17,1},{2,18},{18,2},{3,19},{19,3},{4,20},{20... | collective-permute-start | bytes 7077896 | tf_op jit(solution)/shard_map/ppermute | solution.py:21
  561.8 126.9 %collective-permute-start.88 = (bf16[768,1536]{1,0:T(8,128)(2,1)}, bf16[768,1536]{1,0:T(8,128)(2,1)}, u32[]{:S(2)}, u32[]{:S(2)}) collective-permute-start(bf16[768,1536]{1,0:T(8,128)(2,1)} %multiply_convert_fusion.3), channel_id=1, source_target_pairs={{0,16},{16,0},{1,17},{17,1},{2,18},{18,2},{3,19},{19,3},{4,20},{20... | collective-permute-start | bytes 7077896 | tf_op jit(solution)/shard_map/ppermute | solution.py:21
  562.7 44.9 %collective-permute-start.47 = (bf16[512,768]{1,0:T(8,128)(2,1)}, bf16[512,768]{1,0:T(8,128)(2,1)}, u32[]{:S(2)}, u32[]{:S(2)}) collective-permute-start(bf16[512,768]{1,0:T(8,128)(2,1)} %get-tuple-element.33), channel_id=1, source_target_pairs={{0,4},{4,8},{8,12},{1,5},{5,9},{9,13},{2,6},{6,10},{10,14},{3,7},{... | collective-permute-start | bytes 2359304 | tf_op jit(solution)/shard_map/ppermute | solution.py:55
  607.6 55.1 %collective-permute-start.69 = (bf16[512,768]{1,0:T(8,128)(2,1)}, bf16[512,768]{1,0:T(8,128)(2,1)}, u32[]{:S(2)}, u32[]{:S(2)}) collective-permute-start(bf16[512,768]{1,0:T(8,128)(2,1)} %get-tuple-element.15), channel_id=1, source_target_pairs={{0,4},{4,8},{8,12},{1,5},{5,9},{9,13},{2,6},{6,10},{10,14},{3,7},{... | collective-permute-start | bytes 2359304 | tf_op jit(solution)/shard_map/ppermute | solution.py:55
  619.0 43.8 %collective-permute-start.72 = (bf16[512,768]{1,0:T(8,128)(2,1)}, bf16[512,768]{1,0:T(8,128)(2,1)}, u32[]{:S(2)}, u32[]{:S(2)}) collective-permute-start(bf16[512,768]{1,0:T(8,128)(2,1)} %get-tuple-element.16), channel_id=1, source_target_pairs={{4,0},{8,4},{12,8},{5,1},{9,5},{13,9},{6,2},{10,6},{14,10},{7,3},{... | collective-permute-start | bytes 2359304 | tf_op jit(solution)/shard_map/ppermute | solution.py:56
  623.6 47.5 %collective-permute-start.59 = (bf16[512,768]{1,0:T(8,128)(2,1)}, bf16[512,768]{1,0:T(8,128)(2,1)}, u32[]{:S(2)}, u32[]{:S(2)}) collective-permute-start(bf16[512,768]{1,0:T(8,128)(2,1)} %fusion.93), channel_id=1, source_target_pairs={{4,0},{8,4},{12,8},{5,1},{9,5},{13,9},{6,2},{10,6},{14,10},{7,3},{... | collective-permute-start | bytes 2359304 | tf_op jit(solution)/shard_map/ppermute | solution.py:43
  650.3 22.1 %collective-permute-start.58 = (bf16[512,768]{1,0:T(8,128)(2,1)}, bf16[512,768]{1,0:T(8,128)(2,1)}, u32[]{:S(2)}, u32[]{:S(2)}) collective-permute-start(bf16[512,768]{1,0:T(8,128)(2,1)} %fusion.93), channel_id=1, source_target_pairs={{0,4},{4,8},{8,12},{1,5},{5,9},{9,13},{2,6},{6,10},{10,14},{3,7},{... | collective-permute-start | bytes 2359304 | tf_op jit(solution)/shard_map/ppermute | solution.py:42
  665.2 31.1 %collective-permute-start.78 = (bf16[512,768]{1,0:T(8,128)(2,1)S(1)}, bf16[512,768]{1,0:T(8,128)(2,1)S(1)}, u32[]{:S(2)}, u32[]{:S(2)}) collective-permute-start(bf16[512,768]{1,0:T(8,128)(2,1)S(1)} %fusion.106), channel_id=1, source_target_pairs={{4,0},{8,4},{12,8},{5,1},{9,5},{13,9},{6,2},{10,6},{14,10},{7,3},{... | collective-permute-start | bytes 2359304 | tf_op jit(solution)/shard_map/ppermute | solution.py:43
  666.5 31.2 %collective-permute-start.77 = (bf16[512,768]{1,0:T(8,128)(2,1)S(1)}, bf16[512,768]{1,0:T(8,128)(2,1)S(1)}, u32[]{:S(2)}, u32[]{:S(2)}) collective-permute-start(bf16[512,768]{1,0:T(8,128)(2,1)S(1)} %fusion.106), channel_id=1, source_target_pairs={{0,4},{4,8},{8,12},{1,5},{5,9},{9,13},{2,6},{6,10},{10,14},{3,7},{... | collective-permute-start | bytes 2359304 | tf_op jit(solution)/shard_map/ppermute | solution.py:42
  671.1 27.3 %collective-permute-start.60 = (bf16[512,768]{1,0:T(8,128)(2,1)}, bf16[512,768]{1,0:T(8,128)(2,1)S(1)}, u32[]{:S(2)}, u32[]{:S(2)}) collective-permute-start(bf16[512,768]{1,0:T(8,128)(2,1)} %collective-permute-done.59), channel_id=1, source_target_pairs={{4,0},{8,4},{5,1},{9,5},{6,2},{10,6},{7,3},{11,7},{20,16},{24,20},... | collective-permute-start | bytes 2359304 | tf_op jit(solution)/shard_map/ppermute | solution.py:43
  672.4 27.3 %collective-permute-start.62 = (bf16[512,768]{1,0:T(8,128)(2,1)}, bf16[512,768]{1,0:T(8,128)(2,1)S(1)}, u32[]{:S(2)}, u32[]{:S(2)}) collective-permute-start(bf16[512,768]{1,0:T(8,128)(2,1)} %collective-permute-done.58), channel_id=1, source_target_pairs={{4,8},{8,12},{5,9},{9,13},{6,10},{10,14},{7,11},{11,15},{20,24},{2... | collective-permute-start | bytes 2359304 | tf_op jit(solution)/shard_map/ppermute | solution.py:42
  696.3 22.5 %collective-permute-start.79 = (bf16[512,768]{1,0:T(8,128)(2,1)S(1)}, bf16[512,768]{1,0:T(8,128)(2,1)S(1)}, u32[]{:S(2)}, u32[]{:S(2)}) collective-permute-start(bf16[512,768]{1,0:T(8,128)(2,1)S(1)} %collective-permute-done.78), channel_id=1, source_target_pairs={{4,0},{8,4},{5,1},{9,5},{6,2},{10,6},{7,3},{11,7},{20,16},{24,20},... | collective-permute-start | bytes 2359304 | tf_op jit(solution)/shard_map/ppermute | solution.py:43
  697.7 22.4 %collective-permute-start.81 = (bf16[512,768]{1,0:T(8,128)(2,1)S(1)}, bf16[512,768]{1,0:T(8,128)(2,1)S(1)}, u32[]{:S(2)}, u32[]{:S(2)}) collective-permute-start(bf16[512,768]{1,0:T(8,128)(2,1)S(1)} %collective-permute-done.77), channel_id=1, source_target_pairs={{4,8},{8,12},{5,9},{9,13},{6,10},{10,14},{7,11},{11,15},{20,24},{2... | collective-permute-start | bytes 2359304 | tf_op jit(solution)/shard_map/ppermute | solution.py:42
  698.4 32.5 %collective-permute-start.61 = (bf16[512,768]{1,0:T(8,128)(2,1)S(1)}, bf16[512,768]{1,0:T(8,128)(2,1)S(1)}, u32[]{:S(2)}, u32[]{:S(2)}) collective-permute-start(bf16[512,768]{1,0:T(8,128)(2,1)S(1)} %collective-permute-done.60), channel_id=1, source_target_pairs={{4,0},{5,1},{6,2},{7,3},{20,16},{21,17},{22,18},{23,19}} | collective-permute-start | bytes 2359304 | tf_op jit(solution)/shard_map/ppermute | solution.py:43
  699.7 31.3 %collective-permute-start.63 = (bf16[512,768]{1,0:T(8,128)(2,1)S(1)}, bf16[512,768]{1,0:T(8,128)(2,1)S(1)}, u32[]{:S(2)}, u32[]{:S(2)}) collective-permute-start(bf16[512,768]{1,0:T(8,128)(2,1)S(1)} %collective-permute-done.62), channel_id=1, source_target_pairs={{8,12},{9,13},{10,14},{11,15},{24,28},{25,29},{26,30},{27,31}} | collective-permute-start | bytes 2359304 | tf_op jit(solution)/shard_map/ppermute | solution.py:42
  718.8 32.9 %collective-permute-start.80 = (bf16[512,768]{1,0:T(8,128)(2,1)S(1)}, bf16[512,768]{1,0:T(8,128)(2,1)S(1)}, u32[]{:S(2)}, u32[]{:S(2)}) collective-permute-start(bf16[512,768]{1,0:T(8,128)(2,1)S(1)} %collective-permute-done.79), channel_id=1, source_target_pairs={{4,0},{5,1},{6,2},{7,3},{20,16},{21,17},{22,18},{23,19}} | collective-permute-start | bytes 2359304 | tf_op jit(solution)/shard_map/ppermute | solution.py:43
  720.1 31.7 %collective-permute-start.82 = (bf16[512,768]{1,0:T(8,128)(2,1)S(1)}, bf16[512,768]{1,0:T(8,128)(2,1)S(1)}, u32[]{:S(2)}, u32[]{:S(2)}) collective-permute-start(bf16[512,768]{1,0:T(8,128)(2,1)S(1)} %collective-permute-done.81), channel_id=1, source_target_pairs={{8,12},{9,13},{10,14},{11,15},{24,28},{25,29},{26,30},{27,31}} | collective-permute-start | bytes 2359304 | tf_op jit(solution)/shard_map/ppermute | solution.py:42
  738.7 31.8 %collective-permute-start.83 = (bf16[1536,768]{1,0:T(8,128)(2,1)S(1)}, bf16[1536,768]{1,0:T(8,128)(2,1)S(1)}, u32[]{:S(2)}, u32[]{:S(2)}) collective-permute-start(bf16[1536,768]{1,0:T(8,128)(2,1)S(1)} %multiply_convert_fusion), channel_id=1, source_target_pairs={{0,16},{16,0},{1,17},{17,1},{2,18},{18,2},{3,19},{19,3},{4,20},{20... | collective-permute-start | bytes 7077896 | tf_op jit(solution)/shard_map/ppermute | solution.py:21
  850.8 38.0 %collective-permute-start.85 = (bf16[2,1,256,1536]{3,2,0,1:T(8,128)(2,1)S(1)}, bf16[2,1,256,1536]{3,2,0,1:T(8,128)(2,1)S(1)}, u32[]{:S(2)}, u32[]{:S(2)}) collective-permute-start(bf16[2,1,256,1536]{3,2,0,1:T(8,128)(2,1)S(1)} %fusion.107), channel_id=1, source_target_pairs={{0,2},{1,3},{2,0},{3,1},{4,6},{5,7},{6,4},{7,5},{8,10},{9,11},{10,... | collective-permute-start | bytes 4718600 | tf_op jit(solution)/shard_map/ppermute | solution.py:78
  857.5 54.1 %collective-permute-start.87 = (bf16[1536,768]{1,0:T(8,128)(2,1)S(1)}, bf16[1536,768]{1,0:T(8,128)(2,1)S(1)}, u32[]{:S(2)}, u32[]{:S(2)}) collective-permute-start(bf16[1536,768]{1,0:T(8,128)(2,1)S(1)} %copy-done.5), channel_id=1, source_target_pairs={{0,16},{16,0},{1,17},{17,1},{2,18},{18,2},{3,19},{19,3},{4,20},{20... | collective-permute-start | bytes 7077896 | tf_op jit(solution)/shard_map/ppermute | solution.py:21
  889.6 38.0 %collective-permute-start.86 = (bf16[256,1536]{1,0:T(8,128)(2,1)S(1)}, bf16[256,1536]{1,0:T(8,128)(2,1)S(1)}, u32[]{:S(2)}, u32[]{:S(2)}) collective-permute-start(bf16[256,1536]{1,0:T(8,128)(2,1)S(1)} %fusion.110), channel_id=1, source_target_pairs={{0,16},{16,0},{1,17},{17,1},{2,18},{18,2},{3,19},{19,3},{4,20},{20... | collective-permute-start | bytes 2359304 | tf_op jit(solution)/shard_map/ppermute | solution.py:21
  (105 other events, 1800.1 us)
Sparse Core Ops, SparseCore 0:
  30.5 47.8 all-gather.2
  377.3 45.2 all-gather.4
